TPU v7x, 256 devices: a whole 4x4x8 slice. The times are simulated.
256 devices in a mesh: mom: 8 (over z_lo, x), pts: 32 (over y, z_hi, core).
Axes of the slice: x: 4, y: 4, z: 8 (z_hi: 4, z_lo: 2; z = z_hi * 2 + z_lo), core: 2. Of those that a mesh axis runs over, the one named last changes fastest.
Arguments:
- amplitudes: bfloat16 [2, 2, 1, 256, 64, 128], P(None, None, None, 'mom'), may hold values from -6 to 6
- val_orbitals: bfloat16 [2, 256, 64, 512], P(None, 'mom'), may hold values from -0.25 to 0.25
- cond_orbitals: bfloat16 [2, 256, 512, 128], P(None, 'mom', 'pts'), may hold values from -0.25 to 0.25
- screened: bfloat16 [2, 256, 512, 512], P(None, None, ('pts', 'mom')), may hold values from -12 to 12
- val_energy: float32 [256, 64], P('mom', 'pts'), may hold values from -2 to -0.5
- cond_energy: float32 [256, 128], P('mom'), may hold values from 0.5 to 2
- grid_of_slot: int32 [256], replicated, may hold values from 0 to 255, as said below
- opposite_slot: int32 [256], P('mom'), may hold values from 0 to 255, as said below
Outputs:
- applied: float32 [2, 2, 1, 256, 64, 128], P(None, None, None, 'mom', 'pts')
Inputs may be any that keep to these rules, and one draw needn't show every extreme that they name: `grid_of_slot`: a permutation of the grid indices. opposite_slot[s] is the slot whose grid index is 255 - grid_of_slot[s]; it is never s, and s and opposite_slot[s] lie in aligned blocks of 32 slots whose first slots differ by 128.
All inputs are finite; a program needn't handle non-finite values.
Results may differ from a plain program's by a relative error of at most 0.006.
Values may be sent and summed in bfloat16 or wider, within the bound.
A program may use at most 128 MiB of HBM per device.

v0:
```python
import math
import jax
import jax.numpy as jnp
from jax import lax
from jax.sharding import PartitionSpec as P


def partner_2(value, axis, apart):
    mask = 2**apart
    pairs = [(source, source ^ mask) for source in range(lax.axis_size(axis))]
    return lax.ppermute(value, axis, pairs)


def complex_mix(formula, left, right, left_sign, right_sign):
    real_real = jnp.einsum(formula, left[0], right[0], preferred_element_type=jnp.float32)
    imag_imag = jnp.einsum(formula, left[1], right[1], preferred_element_type=jnp.float32)
    real_imag = jnp.einsum(formula, left[0], right[1], preferred_element_type=jnp.float32)
    imag_real = jnp.einsum(formula, left[1], right[0], preferred_element_type=jnp.float32)
    return jnp.stack(
        [
            real_real - left_sign * right_sign * imag_imag,
            right_sign * real_imag + left_sign * imag_real,
        ]
    )


def on_device(
    amplitudes,
    val_orbitals,
    cond_orbitals,
    screened,
    val_energy,
    cond_energy,
    grid_of_slot,
    opposite_slot,
):
    slots_here = opposite_slot.shape[0]
    total_slots = grid_of_slot.shape[0]
    rows_here = val_energy.shape[1]
    frequency = jnp.arange(total_slots, dtype=jnp.int32)
    phases = frequency[:, None] * grid_of_slot[None, :] % total_slots
    angles = phases.astype(jnp.float32) * (2.0 * math.pi / total_slots)
    cosine_table = jnp.cos(angles).astype(jnp.bfloat16)
    sine_table = jnp.sin(angles).astype(jnp.bfloat16)
    half_product = complex_mix("bnkvc,kuc->bnkvu", amplitudes, cond_orbitals, 1.0, 1.0).astype(
        jnp.bfloat16
    )
    pair_values = complex_mix("bnkvu,kvm->bnkum", half_product, val_orbitals, 1.0, -1.0).astype(
        jnp.bfloat16
    )
    flattened = pair_values.reshape(pair_values.shape[:4] + (-1,))
    weights = screened.reshape(2, total_slots, -1)
    inverse_count = 1.0 / total_slots
    whole_k = lax.all_to_all(flattened, "mom", split_axis=4, concat_axis=3, tiled=True)
    spec_real = jnp.einsum(
        "fs,bnsc->bnfc", cosine_table, whole_k[0], preferred_element_type=jnp.float32
    ) + jnp.einsum("fs,bnsc->bnfc", sine_table, whole_k[1], preferred_element_type=jnp.float32)
    spec_imag = jnp.einsum(
        "fs,bnsc->bnfc", cosine_table, whole_k[1], preferred_element_type=jnp.float32
    ) - jnp.einsum("fs,bnsc->bnfc", sine_table, whole_k[0], preferred_element_type=jnp.float32)
    prod_real = (weights[0] * spec_real - weights[1] * spec_imag).astype(jnp.bfloat16)
    prod_imag = (weights[0] * spec_imag + weights[1] * spec_real).astype(jnp.bfloat16)
    back_real = (
        jnp.einsum("fs,bnfc->bnsc", cosine_table, prod_real, preferred_element_type=jnp.float32)
        - jnp.einsum("fs,bnfc->bnsc", sine_table, prod_imag, preferred_element_type=jnp.float32)
    ) * inverse_count
    back_imag = (
        jnp.einsum("fs,bnfc->bnsc", cosine_table, prod_imag, preferred_element_type=jnp.float32)
        + jnp.einsum("fs,bnfc->bnsc", sine_table, prod_real, preferred_element_type=jnp.float32)
    ) * inverse_count
    field_pts = lax.all_to_all(
        jnp.stack([back_real, back_imag]).astype(jnp.bfloat16),
        "mom",
        split_axis=3,
        concat_axis=4,
        tiled=True,
    )
    field_pts = field_pts.reshape(pair_values.shape)
    weighted = complex_mix("bnkum,kvm->bnkvu", field_pts, val_orbitals, 1.0, 1.0).astype(
        jnp.bfloat16
    )
    band_terms = complex_mix("bnkvu,kuc->bnkvc", weighted, cond_orbitals, 1.0, -1.0)
    band_values = lax.psum_scatter(band_terms, "pts", scatter_dimension=4, tiled=True)
    top_bit = lax.axis_size("mom").bit_length() - 2
    partner = partner_2(band_values.astype(jnp.bfloat16), "mom", top_bit).astype(band_values.dtype)
    mirrored = jnp.take(partner, opposite_slot % slots_here, axis=3)
    start_row = lax.axis_index("pts") * rows_here
    own_rows = lax.dynamic_slice_in_dim(amplitudes, start_row, rows_here, 4).astype(jnp.float32)
    energy_gap = cond_energy[:, None, :] - val_energy[:, :, None]
    result_real = energy_gap * own_rows[0, 0] - band_values[0, 0] - mirrored[0, 1]
    result_imag = energy_gap * own_rows[1, 0] - band_values[1, 0] + mirrored[1, 1]
    anti_real = -energy_gap * own_rows[0, 1] + band_values[0, 1] + mirrored[0, 0]
    anti_imag = -energy_gap * own_rows[1, 1] + band_values[1, 1] - mirrored[1, 0]
    return jnp.stack([jnp.stack([result_real, anti_real]), jnp.stack([result_imag, anti_imag])])


def solution(mesh):
    in_specs = (
        P(None, None, None, "mom", None, None),
        P(None, "mom", None, None),
        P(None, "mom", "pts", None),
        P(None, None, ("pts", "mom"), None),
        P("mom", "pts"),
        P("mom", None),
        P(),
        P("mom"),
    )
    out_specs = P(None, None, None, "mom", "pts", None)
    return jax.shard_map(
        on_device, mesh=mesh, in_specs=in_specs, out_specs=out_specs, check_vma=False
    )
```

profile of v0, /device:TPU:2, one launch (start us, length us, event | category | flops | bytes accessed | tf_op | source)
XLA Modules:
  0.0 286.6 jit_solution(13320353008249521485)
XLA Ops:
  6.5 1.8 fusion.151
  13.4 4.9 %copy.167 = bf16[2,1,32,16,512]{2,0,4,3,1:T(2,128)(2,1)} copy(bf16[2,1,32,16,512]{4,3,0,2,1:T(8,128)(2,1)S(1)} %fusion.24) | data formatting | bytes 2097152 | tf_op jit(solution)/shard_map/stack | solution.py:19
  18.3 2.1 fusion.27
  20.4 4.9 %copy.168 = bf16[2,1,32,16,512]{2,0,4,3,1:T(2,128)(2,1)} copy(bf16[2,1,32,16,512]{4,3,0,2,1:T(8,128)(2,1)S(1)} %fusion.27) | data formatting | bytes 2097152 | tf_op jit(solution)/shard_map/stack | solution.py:19
  25.3 16.3 %fusion.153 = bf16[8192,1,2,2,32]{4,3,2,1,0:T(2,128)(2,1)} fusion(bf16[1,2,1,32,8192]{3,1,0,2,4:T(2,128)(2,1)} %bitcast.313, bf16[1,2,1,32,8192]{3,1,0,2,4:T(2,128)(2,1)} %bitcast.312), kind=kLoop, calls=%fused_computation.180 | loop fusion | flops 1048576 | bytes 4194304
  41.7 11.2 %reshape.527 = bf16[8,2,65536]{2,1,0:T(2,128)(2,1)} reshape(bf16[8192,1,2,2,32]{4,3,2,1,0:T(2,128)(2,1)} %fusion.153) | data formatting | bytes 4194304
  52.9 6.3 %all-to-all-start = ((bf16[8,2,65536]{2,1,0:T(2,128)(2,1)}), bf16[8,2,65536]{2,1,0:T(2,128)(2,1)S(1)}, u32[]{:S(2)}, u32[]{:S(2)}) async-start(bf16[8,2,65536]{2,1,0:T(2,128)(2,1)} %reshape.527), calls=%async_computation | async-start | bytes 4194304 | tf_op jit(solution)/shard_map/all_to_all | solution.py:54
  59.2 2.1 slice_convert_fusion.1
  61.2 1.5 copy.166
  62.7 2.3 copy.170
  65.0 19.0 %all-to-all-done = bf16[8,2,65536]{2,1,0:T(2,128)(2,1)S(1)} async-done(((bf16[8,2,65536]{2,1,0:T(2,128)(2,1)}), bf16[8,2,65536]{2,1,0:T(2,128)(2,1)S(1)}, u32[]{:S(2)}, u32[]{:S(2)}) %all-to-all-start) | async-done | bytes 2097184 | tf_op jit(solution)/shard_map/all_to_all | solution.py:54
  84.0 6.5 %reshape.528 = bf16[8192,1,2,2,32]{4,3,2,1,0:T(2,128)(2,1)} reshape(bf16[8,2,65536]{2,1,0:T(2,128)(2,1)S(1)} %all-to-all-done) | data formatting | bytes 4194304
  90.6 11.9 %copy.169 = bf16[2,2,1,32,8,1024]{5,4,3,1,0,2:T(8,128)(2,1)S(1)} copy(bf16[2,2,1,32,8,1024]{3,1,0,5,4,2:T(2,128)(2,1)} %bitcast.311) | data formatting | bytes 4194304 | tf_op jit(solution)/shard_map/all_to_all | solution.py:54
  103.8 1.4 fusion.92
  105.3 1.4 fusion.94
  106.7 1.4 convolution_subtract_fusion
  108.1 2.5 fusion.63
  110.6 1.4 fusion.90
  112.0 1.4 fusion.88
  113.3 1.4 fusion.30
  114.7 1.4 fusion.31
  116.3 4.1 %copy.142 = bf16[2,2,1,256,1024]{4,1,2,0,3:T(2,128)(2,1)} copy(bf16[2,2,1,256,1024]{3,4,1,2,0:T(8,128)(2,1)S(1)} %pad_maximum_fusion.2) | data formatting | bytes 4194304 | tf_op jit(solution)/shard_map/stack | solution.py:72
  120.4 30.3 %all_to_all.30 = bf16[2,2,1,256,1024]{4,1,2,0,3:T(2,128)(2,1)S(1)} all-to-all(bf16[2,2,1,256,1024]{4,1,2,0,3:T(2,128)(2,1)} %copy.142), channel_id=1, replica_groups=mesh['mom'=8,'pts'=32] {'mom'}, dimensions={3} | all-to-all | bytes 4194304 | tf_op jit(solution)/shard_map/all_to_all | solution.py:71
  151.4 1.2 fusion.149
  153.6 3.2 %fusion.4 = f32[32,2,16,64]{3,2,1,0:T(8,128)} fusion(bf16[2,32,16,512]{3,2,0,1:T(8,128)(2,1)S(1)} %reshape.505, bf16[2,32,64,512]{3,2,1,0:T(8,128)(2,1)} %param.9), kind=kOutput, calls=%fused_computation.12 | convolution fusion | flops 67108864 | bytes 3407872 | tf_op jit(solution)/shard_map/bnkum,kvm->bnkvu/dot_general | solution.py:18
  157.7 2.3 fusion.6
  160.0 2.3 fusion.56
  163.3 1.2 copy-done.1
  166.8 4.4 %copy.146 = f32[2,2,1,32,64,128]{5,3,2,1,0,4:T(8,128)} copy(f32[2,2,1,32,64,128]{5,4,1,3,2,0:T(8,128)S(1)} %pad_maximum_fusion.1) | data formatting | bytes 8388608 | tf_op jit(solution)/shard_map/stack | solution.py:19
  172.0 1.0 dynamic-slice_convert_fusion
  173.0 99.4 %reduce-scatter.2.cloned.1.call-done = f32[2,2,1,32,2,128]{5,3,2,1,0,4:T(8,128)} async-done(((f32[2,2,1,32,64,128]{5,3,2,1,0,4:T(8,128)}), f32[2,2,1,32,2,128]{5,3,2,1,0,4:T(8,128)}) %reduce-scatter.2.cloned.1.call-update) | async-done | bytes 131088 | tf_op jit(solution)/shard_map/reduce_scatter | solution.py:83
  274.5 3.3 %collective-permute-done = bf16[2,2,1,32,2,128]{5,4,3,1,0,2:T(2,128)(2,1)S(1)} collective-permute-done((bf16[2,2,1,32,2,128]{5,4,3,1,0,2:T(2,128)(2,1)S(1)}, bf16[2,2,1,32,2,128]{5,4,3,1,0,2:T(2,128)(2,1)S(1)}, u32[]{:S(2)}, u32[]{:S(2)}) %collective-permute-start) | collective-permute-done | bytes 65568 | tf_op jit(solution)/shard_map/ppermute | solution.py:11
  (61 shorter events, 17.3 us)
Async XLA Ops:
  6.5 1.8 copy-start.4
  9.2 2.8 copy-start
  11.1 1.4 copy-start.5
  52.9 6.3 %copy-start.7 = (bf16[2,256,2,512]{3,2,1,0:T(2,128)(2,1)S(1)}, bf16[2,256,2,512]{3,2,1,0:T(2,128)(2,1)}, u32[]{:S(2)}) copy-start(bf16[2,256,2,512]{3,2,1,0:T(2,128)(2,1)} %param.11) | copy-start | bytes 3145732
  52.9 31.2 %all-to-all-start = ((bf16[8,2,65536]{2,1,0:T(2,128)(2,1)}), bf16[8,2,65536]{2,1,0:T(2,128)(2,1)S(1)}, u32[]{:S(2)}, u32[]{:S(2)}) async-start(bf16[8,2,65536]{2,1,0:T(2,128)(2,1)} %reshape.527), calls=%async_computation | async-start | bytes 4194304 | tf_op jit(solution)/shard_map/all_to_all | solution.py:54
  59.2 213.2 %reduce-scatter.2.cloned.1.call-start = ((), (), s32[]{:S(2)}) async-start(), calls=%async_computation.3 | async-start | bytes 4325376 | tf_op jit(solution)/shard_map/reduce_scatter | solution.py:83
  102.7 1.2 copy-start.9
  106.7 1.4 copy-start.2
  153.6 3.2 %copy-start.3 = (bf16[1,2,1,32,8,1024]{5,3,4,1,0,2:T(8,128)(2,1)S(1)}, bf16[1,2,1,32,8,1024]{5,3,4,1,0,2:T(8,128)(2,1)}, u32[]{:S(2)}) copy-start(bf16[1,2,1,32,8,1024]{5,3,4,1,0,2:T(8,128)(2,1)} %get-tuple-element.10) | copy-start | bytes 3145732
  162.3 2.2 copy-start.1
  162.3 2.3 copy-start.6
  171.2 0.7 copy-start.10
  171.2 0.8 copy-start.11
  171.2 107.5 %copy-start.8 = (f32[32,128]{1,0:T(8,128)S(1)}, f32[32,128]{1,0:T(8,128)}, u32[]{:S(2)}) copy-start(f32[32,128]{1,0:T(8,128)} %param.13) | copy-start | bytes 49156
  273.4 4.4 %collective-permute-start = (bf16[2,2,1,32,2,128]{5,4,3,1,0,2:T(2,128)(2,1)S(1)}, bf16[2,2,1,32,2,128]{5,4,3,1,0,2:T(2,128)(2,1)S(1)}, u32[]{:S(2)}, u32[]{:S(2)}) collective-permute-start(bf16[2,2,1,32,2,128]{5,4,3,1,0,2:T(2,128)(2,1)S(1)} %copy.199), channel_id=1, source_target_pairs={{0,128},{32,160},{64,192},{96,224},{128,0},{160,32},{192,64},{224,... | collective-permute-start | bytes 196616 | tf_op jit(solution)/shard_map/ppermute | solution.py:11
Sparse Core Ops, SparseCore 0:
  171.3 101.0 reduce-scatter.1
where the time goes:
time: 288 us; the launch traced here: 287 us
  waiting for transfers between devices  122 us (42%)
  local copies, waits for them, and re-layouts  63.2 us (22%)
  blocking collectives  30.3 us (11%)
  matrix products  29.7 us (10%)
  other arithmetic  21.4 us (7%)
  between operations  13.7 us (5%)
  starting transfers between devices  6.58 us (2%)
    reduce_scatter x1, waiting for transfers between devices, on_device(): lax.psum_scatter(band_terms, 'pts', scatter_dimension=4, tiled=True)  99.4 us
    all_to_all x1, blocking collectives, on_device(): lax.all_to_all(jnp.stack([back_real, back_imag]).astype(jnp.bfloat16), 'm...  30.3 us
    unnamed x27, local copies, waits for them, and re-layouts  19.8 us
    all_to_all x1, waiting for transfers between devices, on_device(): lax.all_to_all(flattened, 'mom', split_axis=4, concat_axis=3, tiled=True)  19 us
    unnamed x1, other arithmetic  16.3 us
    another operation x3, local copies, waits for them, and re-layouts, complex_mix(): jnp.stack([real_real - left_sign * right_sign * imag_imag, right_sign * r...  14.2 us
    all_to_all x1, local copies, waits for them, and re-layouts, on_device(): lax.all_to_all(flattened, 'mom', split_axis=4, concat_axis=3, tiled=True)  11.9 us
    all_to_all x1, starting transfers between devices, on_device(): lax.all_to_all(flattened, 'mom', split_axis=4, concat_axis=3, tiled=True)  6.32 us
  transfers between devices with their start and end apart: 3, of which 3 were waited for; matrix products, arithmetic and copies ran while one was open for 3% of the time, Pallas kernels for 0%

commit v1 on v0

--- a/solution.py
+++ b/solution.py
@@ -51,7 +51,10 @@
     flattened = pair_values.reshape(pair_values.shape[:4] + (-1,))
     weights = screened.reshape(2, total_slots, -1)
     inverse_count = 1.0 / total_slots
-    whole_k = lax.all_to_all(flattened, "mom", split_axis=4, concat_axis=3, tiled=True)
+    whole_k = jnp.concatenate(
+        lax.all_to_all(jnp.stack(jnp.split(flattened, lax.axis_size("mom"), axis=4)), "mom", 0, 0),
+        axis=3,
+    )
     spec_real = jnp.einsum(
         "fs,bnsc->bnfc", cosine_table, whole_k[0], preferred_element_type=jnp.float32
     ) + jnp.einsum("fs,bnsc->bnfc", sine_table, whole_k[1], preferred_element_type=jnp.float32)

time: 288 us -> 243 us (0.84)
  local copies, waits for them, and re-layouts: 63.2 us -> 33.7 us
  other arithmetic: 21.4 us -> 5.05 us
    unnamed x1 -> x0, other arithmetic: 16.3 us -> none
    unnamed x27 -> x33, local copies, waits for them, and re-layouts: 19.8 us -> 8.08 us
    all_to_all x1, local copies, waits for them, and re-layouts: 11.9 us -> 0.17 us  [on_device(): lax.all_to_all(jnp.stack(jnp.split(flattened, lax.axis_size('mom'), axis=...]
    another operation x3 -> x4, local copies, waits for them, and re-layouts: 14.2 us -> 8.63 us  [complex_mix(): jnp.stack([real_real - left_sign * right_sign * imag_imag, right_sign * r...]
where the time goes in v1:
time: 243 us
  waiting for transfers between devices  122 us (50%)
  local copies, waits for them, and re-layouts  33.7 us (14%)
  matrix products  31.4 us (13%)
  blocking collectives  30.3 us (12%)
  between operations  13.7 us (6%)
  starting transfers between devices  6.6 us (3%)
  other arithmetic  5.05 us (2%)
    reduce_scatter x1, waiting for transfers between devices, on_device(): lax.psum_scatter(band_terms, 'pts', scatter_dimension=4, tiled=True)  99.5 us
    all_to_all x1, blocking collectives, on_device(): lax.all_to_all(jnp.stack([back_real, back_imag]).astype(jnp.bfloat16), 'm...  30.3 us
    all_to_all x1, waiting for transfers between devices, on_device(): lax.all_to_all(jnp.stack(jnp.split(flattened, lax.axis_size('mom'), axis=...  19.1 us
    another operation x4, local copies, waits for them, and re-layouts, complex_mix(): jnp.stack([real_real - left_sign * right_sign * imag_imag, right_sign * r...  8.63 us
    unnamed x33, local copies, waits for them, and re-layouts  8.08 us
    dot_general x4, matrix products, complex_mix(): jnp.einsum(formula, left[1], right[1], preferred_element_type=jnp.float32)  6.83 us
    all_to_all x1, starting transfers between devices, on_device(): lax.all_to_all(jnp.stack(jnp.split(flattened, lax.axis_size('mom'), axis=...  6.32 us
    dot_general x4, matrix products, complex_mix(): jnp.einsum(formula, left[1], right[0], preferred_element_type=jnp.float32)  5.03 us
  transfers between devices with their start and end apart: 3, of which 3 were waited for; matrix products, arithmetic and copies ran while one was open for 3% of the time, Pallas kernels for 0%

profile of v1, /device:TPU:2, one launch (start us, length us, event | category | flops | bytes accessed | tf_op | source)
XLA Modules:
  0.0 242.8 jit_solution(7582735988392443048)
XLA Ops:
  6.5 1.8 fusion.159
  10.2 0.9 fusion.54
  11.1 0.9 fusion.55
  12.9 1.4 fusion.27
  14.4 1.8 stack.80
  16.2 3.1 %fusion.24 = bf16[2,1,32,16,512]{4,3,0,2,1:T(8,128)(2,1)} fusion(f32[32,2,16,512]{3,2,1,0:T(8,128)S(1)} %fusion.10, bf16[2,32,64,16]{2,3,0,1:T(8,128)(2,1)} %copy-done.5, bf16[2,32,64,512]{3,2,1,0:T(8,128)(2,1)} %param.9), kind=kOutput, calls=%fused_computation.36 | convolution fusion | flops 68681728 | bytes 5505024 | tf_op jit(solution)/shard_map/bnkvu,kvm->bnkum/dot_general | solution.py:16
  19.3 1.8 stack.79
  28.1 6.3 %all-to-all-start = ((bf16[8,2,2,1,32,1024]{5,4,2,3,1,0:T(8,128)(2,1)}), bf16[8,2,2,1,32,1024]{5,4,2,3,1,0:T(8,128)(2,1)S(1)}, u32[]{:S(2)}, u32[]{:S(2)}) async-start(bf16[8,2,2,1,32,1024]{5,4,2,3,1,0:T(8,128)(2,1)} %fusion.69), calls=%async_computation | async-start | bytes 4194304 | tf_op jit(solution)/shard_map/all_to_all | solution.py:55
  34.4 2.0 slice_convert_fusion.1
  36.4 1.5 copy.103
  37.9 2.3 copy.104
  40.2 19.1 %all-to-all-done = bf16[8,2,2,1,32,1024]{5,4,2,3,1,0:T(8,128)(2,1)S(1)} async-done(((bf16[8,2,2,1,32,1024]{5,4,2,3,1,0:T(8,128)(2,1)}), bf16[8,2,2,1,32,1024]{5,4,2,3,1,0:T(8,128)(2,1)S(1)}, u32[]{:S(2)}, u32[]{:S(2)}) %all-to-all-start) | async-done | bytes 2097184 | tf_op jit(solution)/shard_map/all_to_all | solution.py:55
  60.1 1.4 fusion.100
  61.5 1.4 fusion.102
  63.0 1.4 convolution_subtract_fusion
  64.4 2.2 fusion.63
  66.6 1.4 fusion.98
  68.0 1.4 fusion.96
  69.4 1.4 fusion.30
  70.8 1.4 fusion.31
  72.4 4.1 %copy.79 = bf16[2,2,1,256,1024]{4,1,2,0,3:T(2,128)(2,1)} copy(bf16[2,2,1,256,1024]{3,4,1,2,0:T(8,128)(2,1)S(1)} %pad_maximum_fusion.1) | data formatting | bytes 4194304 | tf_op jit(solution)/shard_map/stack | solution.py:75
  76.5 30.3 %all_to_all.20 = bf16[2,2,1,256,1024]{4,1,2,0,3:T(2,128)(2,1)S(1)} all-to-all(bf16[2,2,1,256,1024]{4,1,2,0,3:T(2,128)(2,1)} %copy.79), channel_id=1, replica_groups=mesh['mom'=8,'pts'=32] {'mom'}, dimensions={3} | all-to-all | bytes 4194304 | tf_op jit(solution)/shard_map/all_to_all | solution.py:74
  107.5 1.2 fusion.157
  109.6 3.2 %fusion.4 = f32[32,2,16,64]{3,2,1,0:T(8,128)} fusion(bf16[2,32,16,512]{3,2,0,1:T(8,128)(2,1)S(1)} %reshape.510, bf16[2,32,64,512]{3,2,1,0:T(8,128)(2,1)} %param.9), kind=kOutput, calls=%fused_computation.11 | convolution fusion | flops 67108864 | bytes 3407872 | tf_op jit(solution)/shard_map/bnkum,kvm->bnkvu/dot_general | solution.py:18
  113.8 2.3 fusion.6
  116.0 2.3 fusion.56
  119.3 1.2 copy-done.1
  122.9 4.4 %copy.83 = f32[2,2,1,32,64,128]{5,3,2,1,0,4:T(8,128)} copy(f32[2,2,1,32,64,128]{5,4,1,3,2,0:T(8,128)S(1)} %pad_maximum_fusion) | data formatting | bytes 8388608 | tf_op jit(solution)/shard_map/stack | solution.py:19
  128.0 1.0 dynamic-slice_convert_fusion
  129.0 99.5 %reduce-scatter.2.cloned.1.call-done = f32[2,2,1,32,2,128]{5,3,2,1,0,4:T(8,128)} async-done(((f32[2,2,1,32,64,128]{5,3,2,1,0,4:T(8,128)}), f32[2,2,1,32,2,128]{5,3,2,1,0,4:T(8,128)}) %reduce-scatter.2.cloned.1.call-update) | async-done | bytes 131088 | tf_op jit(solution)/shard_map/reduce_scatter | solution.py:86
  228.5 1.0 copy.136
  230.7 3.2 %collective-permute-done = bf16[2,2,1,32,2,128]{5,4,3,1,0,2:T(2,128)(2,1)S(1)} collective-permute-done((bf16[2,2,1,32,2,128]{5,4,3,1,0,2:T(2,128)(2,1)S(1)}, bf16[2,2,1,32,2,128]{5,4,3,1,0,2:T(2,128)(2,1)S(1)}, u32[]{:S(2)}, u32[]{:S(2)}) %collective-permute-start) | collective-permute-done | bytes 65568 | tf_op jit(solution)/shard_map/ppermute | solution.py:11
  (66 shorter events, 20.4 us)
Async XLA Ops:
  6.5 1.8 copy-start.4
  9.2 2.8 %copy-start = (bf16[2,32,64,512]{3,2,1,0:T(8,128)(2,1)S(1)}, bf16[2,32,64,512]{3,2,1,0:T(8,128)(2,1)}, u32[]{:S(2)}) copy-start(bf16[2,32,64,512]{3,2,1,0:T(8,128)(2,1)} %param.9) | copy-start | bytes 12582916
  11.1 1.4 copy-start.5
  28.1 6.3 %copy-start.7 = (bf16[2,256,2,512]{3,2,1,0:T(2,128)(2,1)S(1)}, bf16[2,256,2,512]{3,2,1,0:T(2,128)(2,1)}, u32[]{:S(2)}) copy-start(bf16[2,256,2,512]{3,2,1,0:T(2,128)(2,1)} %param.11) | copy-start | bytes 3145732
  28.1 31.2 %all-to-all-start = ((bf16[8,2,2,1,32,1024]{5,4,2,3,1,0:T(8,128)(2,1)}), bf16[8,2,2,1,32,1024]{5,4,2,3,1,0:T(8,128)(2,1)S(1)}, u32[]{:S(2)}, u32[]{:S(2)}) async-start(bf16[8,2,2,1,32,1024]{5,4,2,3,1,0:T(8,128)(2,1)} %fusion.69), calls=%async_computation | async-start | bytes 4194304 | tf_op jit(solution)/shard_map/all_to_all | solution.py:55
  34.4 194.1 %reduce-scatter.2.cloned.1.call-start = ((), (), s32[]{:S(2)}) async-start(), calls=%async_computation.3 | async-start | bytes 4325376 | tf_op jit(solution)/shard_map/reduce_scatter | solution.py:86
  59.4 0.7 copy-start.9
  62.9 1.4 copy-start.2
  109.6 3.2 %copy-start.3 = (bf16[1,2,1,32,8,1024]{5,3,4,1,0,2:T(8,128)(2,1)S(1)}, bf16[1,2,1,32,8,1024]{5,3,4,1,0,2:T(8,128)(2,1)}, u32[]{:S(2)}) copy-start(bf16[1,2,1,32,8,1024]{5,3,4,1,0,2:T(8,128)(2,1)} %get-tuple-element.10) | copy-start | bytes 3145732
  118.3 2.2 copy-start.1
  118.3 2.3 copy-start.6
  127.2 0.7 copy-start.10
  127.2 0.8 copy-start.11
  127.2 107.6 %copy-start.8 = (f32[32,128]{1,0:T(8,128)S(1)}, f32[32,128]{1,0:T(8,128)}, u32[]{:S(2)}) copy-start(f32[32,128]{1,0:T(8,128)} %param.13) | copy-start | bytes 49156
  229.6 4.4 %collective-permute-start = (bf16[2,2,1,32,2,128]{5,4,3,1,0,2:T(2,128)(2,1)S(1)}, bf16[2,2,1,32,2,128]{5,4,3,1,0,2:T(2,128)(2,1)S(1)}, u32[]{:S(2)}, u32[]{:S(2)}) collective-permute-start(bf16[2,2,1,32,2,128]{5,4,3,1,0,2:T(2,128)(2,1)S(1)} %copy.136), channel_id=1, source_target_pairs={{0,128},{32,160},{64,192},{96,224},{128,0},{160,32},{192,64},{224,... | collective-permute-start | bytes 196616 | tf_op jit(solution)/shard_map/ppermute | solution.py:11
Sparse Core Ops, SparseCore 0:
  127.4 101.1 reduce-scatter.1
